TPU v7x, 32 devices: a whole 2x2x4 slice. The times are simulated.
32 devices in a mesh: gx: 4 (over y, core), gy: 8 (over z, x).
Axes of the slice: x: 2, y: 2, z: 4, core: 2. Of those that a mesh axis runs over, the one named last changes fastest.
Arguments:
- initial_warmth: float32 [128, 128, 256], P('gx', 'gy'), may hold values from -4 to 4
- energy_source_density: float32 [128, 128, 256], P('gx', 'gy'), may hold values from -4 to 4
- baseline_transport_coefficient: float32 [128, 128, 256], P('gx', 'gy'), may hold values from 256 to 1024
Outputs:
- new_temperature: float32 [128, 128, 256], P('gx', 'gy')
All inputs are finite; a program needn't handle non-finite values.
Results may differ from a plain program's by a relative error of at most 0.0003.
Values sent between devices are 32-bit elements; how exact they have to be, the bound alone decides.
A program may use at most 128 MiB of HBM per device.

v0:
```python
import functools

import jax
import jax.numpy as jnp
from jax import lax
from jax.experimental import pallas as pl
from jax.experimental.pallas import tpu as pltpu
from jax.sharding import PartitionSpec as P

MESH = pl.DeviceIdType.MESH
LANES = 128


def kernel(nx, ny, gx, gy, lx, ly, u_hbm, s_hbm, k_hbm, o_hbm,
           field, rhs, xd, xe, xw, yd, ye, yw, yi, hx, hys, hyr,
           zq, zfm, zfp,
           xsend, xrecv, xback, xgot, ycs, ycr, yrs, yrr, yback, ygot, yfw, yfi,
           in_sem, out_sem, hs_sem, hr_sem, xs_sem, xr_sem, xbs_sem, xbr_sem,
           ycs_sem, ycr_sem, yrs_sem, yrr_sem, ybs_sem, ybr_sem):
    rows = nx * ny
    mx = lax.axis_index("gx")
    my = lax.axis_index("gy")

    loads = []
    for a, (src, dst) in enumerate(((u_hbm, field.at[0]), (k_hbm, field.at[1]), (s_hbm, rhs))):
        for h in range(2):
            c = pltpu.make_async_copy(src.at[:, pl.ds(h * LANES, LANES)], dst.at[h], in_sem.at[a, h])
            c.start()
            loads.append(c)

    barrier = pltpu.get_barrier_semaphore()
    for o in range(1, gx):
        pl.semaphore_signal(barrier, inc=1, device_id={"gx": lax.rem(mx + o, gx)}, device_id_type=MESH)
    for o in range(1, gy):
        pl.semaphore_signal(barrier, inc=1, device_id={"gy": lax.rem(my + o, gy)}, device_id_type=MESH)

    for c in loads[:4]:
        c.wait()
    block = 32
    for r in range(0, rows, block):
        u = field[0, :, r:r + block, :]
        field[1, :, r:r + block, :] = field[1, :, r:r + block, :] * (1.0 + 0.5 * u * u)

    def yrow(q, j):
        return [field[q, h, pl.ds(j, nx, stride=ny), :] for h in range(2)]

    for q in range(2):
        for h in range(2):
            hys[0, q, h] = field[q, h, pl.ds(0, nx, stride=ny), :]
            hys[1, q, h] = field[q, h, pl.ds(ny - 1, nx, stride=ny), :]

    pl.semaphore_wait(barrier, gx + gy - 2)

    def halo(axis, me, count, src_first, src_last, recv, base):
        down = pltpu.make_async_remote_copy(
            src_ref=src_first, dst_ref=recv.at[1], send_sem=hs_sem.at[base], recv_sem=hr_sem.at[base],
            device_id={axis: lax.rem(me + count - 1, count)}, device_id_type=MESH)
        up = pltpu.make_async_remote_copy(
            src_ref=src_last, dst_ref=recv.at[0], send_sem=hs_sem.at[base + 1], recv_sem=hr_sem.at[base + 1],
            device_id={axis: lax.rem(me + 1, count)}, device_id_type=MESH)

        @pl.when(me > 0)
        def _():
            down.start()

        @pl.when(me < count - 1)
        def _():
            up.start()

        @pl.when(me == 0)
        def _():
            recv[0] = jnp.zeros(recv.shape[1:], jnp.float32)

        @pl.when(me == count - 1)
        def _():
            recv[1] = jnp.zeros(recv.shape[1:], jnp.float32)

        def wait():
            @pl.when(me > 0)
            def _():
                down.wait_send()
                up.wait_recv()

            @pl.when(me < count - 1)
            def _():
                up.wait_send()
                down.wait_recv()
        return wait

    wait_y = halo("gy", my, gy, hys.at[0], hys.at[1], hyr, 0)
    wait_x = halo("gx", mx, gx, field.at[:, :, pl.ds(0, ny), :],
                  field.at[:, :, pl.ds(rows - ny, ny), :], hx, 2)

    for c in loads[4:]:
        c.wait()

    lane = lax.broadcasted_iota(jnp.int32, (block, LANES), 1)

    def prev(a, s):
        if s == LANES:
            return a[1], a[0]
        p0, p1 = pltpu.roll(a[0], s, 1), pltpu.roll(a[1], s, 1)
        return p0, jnp.where(lane < s, p0, p1)

    def nxt(a, s):
        n0, n1 = pltpu.roll(a[0], LANES - s, 1), pltpu.roll(a[1], LANES - s, 1)
        return jnp.where(lane >= LANES - s, n1, n0), n1

    first, last = lane == 0, lane == LANES - 1

    for r in range(0, rows, block):
        at = pl.ds(r, block)
        u = [field[0, h, at, :] for h in range(2)]
        c = [field[1, h, at, :] for h in range(2)]
        up_, cp = prev(u, 1), prev(c, 1)
        un, cn = nxt(u, 1), nxt(c, 1)
        zero = jnp.zeros_like(lane, jnp.float32)
        up_, cp = [jnp.where(first, zero, up_[0]), up_[1]], [jnp.where(first, zero, cp[0]), cp[1]]
        un, cn = [un[0], jnp.where(last, zero, un[1])], [cn[0], jnp.where(last, zero, cn[1])]
        for h in range(2):
            gm, gp = 0.25 * (c[h] + cp[h]), 0.25 * (c[h] + cn[h])
            rhs[h, at, :] = rhs[h, at, :] + 2.0 * (gp * (un[h] - u[h]) - gm * (u[h] - up_[h]))
            if h == 0:
                zq[0, h, at, :] = jnp.where(first, zero, gm)
                zq[1, h, at, :] = gp
                zq[2, h, at, :] = jnp.where(first, 1.0 + gm, 1.0)
            else:
                zq[0, h, at, :] = gm
                zq[1, h, at, :] = jnp.where(last, zero, gp)
                zq[2, h, at, :] = jnp.where(last, 1.0 + gp, 1.0)

    def zfactor(step):
        s = 1 << step
        for r in range(0, rows, block):
            at = pl.ds(r, block)
            qm = [zq[0, h, at, :] for h in range(2)]
            qp = [zq[1, h, at, :] for h in range(2)]
            m = [zq[2, h, at, :] for h in range(2)]
            ib = [1.0 / (m[h] + (qm[h] + qp[h])) for h in range(2)]
            if s == LANES:
                fp0, fm1 = qp[0] * ib[1], qm[1] * ib[0]
                zfm[step, 0, at, :] = fp0
                zfm[step, 1, at, :] = fm1
                zfp[step, 0, at, :] = 1.0 / (m[0] + fp0 * m[1])
                zfp[step, 1, at, :] = 1.0 / (m[1] + fm1 * m[0])
                continue
            ip, inx = prev(ib, s), nxt(ib, s)
            mp, mn = prev(m, s), nxt(m, s)
            qmp, qpn = prev(qm, s), nxt(qp, s)
            for h in range(2):
                fm, fp = qm[h] * ip[h], qp[h] * inx[h]
                zfm[step, h, at, :] = fm
                zfp[step, h, at, :] = fp
                zq[0, h, at, :] = fm * qmp[h]
                zq[1, h, at, :] = fp * qpn[h]
                zq[2, h, at, :] = m[h] + (fm * mp[h] + fp * mn[h])

    wait_y()

    def joined(parts):
        return jnp.concatenate(parts, axis=0)

    up_, cp = joined([hyr[0, 0, 0], hyr[0, 0, 1]]), joined([hyr[0, 1, 0], hyr[0, 1, 1]])
    u, c = joined(yrow(0, 0)), joined(yrow(1, 0))
    gm = 0.25 * (c + cp)
    for j in range(ny):
        if j < ny - 1:
            un, cn = joined(yrow(0, j + 1)), joined(yrow(1, j + 1))
        else:
            un, cn = joined([hyr[1, 0, 0], hyr[1, 0, 1]]), joined([hyr[1, 1, 0], hyr[1, 1, 1]])
        gp = 0.25 * (c + cn)
        t = 2.0 * (gp * (un - u) - gm * (u - up_))
        yw[j] = gm
        if j == ny - 1:
            yw[ny] = gp
        for h in range(2):
            at = pl.ds(j, nx, stride=ny)
            rhs[h, at, :] = rhs[h, at, :] + t[h * nx:(h + 1) * nx]
        up_, u, c, gm = u, un, cn, gp

    wait_x()

    def xrow(q, i):
        return joined([field[q, h, pl.ds(i * ny, ny), :] for h in range(2)])

    def split_send(values, buf, count, per):
        for q, v in enumerate(values):
            for t in range(count):
                buf[t, q] = v[t * per:(t + 1) * per]

    up_, cp = joined([hx[0, 0, 0], hx[0, 0, 1]]), joined([hx[0, 1, 0], hx[0, 1, 1]])
    u, c = xrow(0, 0), xrow(1, 0)
    gm = 0.25 * (c + cp)
    edge_lo = jnp.where(mx == 0, 1.0, 0.0)
    edge_hi = jnp.where(mx == gx - 1, 1.0, 0.0)
    mass, link, dd, sig, d1 = None, None, None, None, None
    for i in range(nx):
        if i < nx - 1:
            un, cn = xrow(0, i + 1), xrow(1, i + 1)
        else:
            un, cn = joined([hx[1, 0, 0], hx[1, 0, 1]]), joined([hx[1, 1, 0], hx[1, 1, 1]])
        gp = 0.25 * (c + cn)
        d = joined([rhs[h, pl.ds(i * ny, ny), :] for h in range(2)])
        d = d + 2.0 * (gp * (un - u) - gm * (u - up_))
        if i == 0:
            mass, link, dd = 1.0 + edge_lo * gm, (1.0 - edge_lo) * gm, d
        else:
            mass, link, dd = 1.0 + w * mass, w * link, d + w * dd
        if i < nx - 1:
            ib = 1.0 / (mass + link + gp)
            w = gp * ib
            e = link * ib
            xd[i], xe[i], xw[i] = dd * ib, e, w
            sig = e * mass if i == 0 else sig + e * mass
            d1 = e * dd if i == 0 else d1 + e * dd
        up_, u, c, gm = u, un, cn, gp
    mass = mass + edge_hi * gm
    split_send((link, mass, sig, dd, d1), xsend, gx, lx)

    def exchange(axis, me, count, src, dst, send_sem, recv_sem):
        copies = []
        for o in range(1, count):
            peer = lax.rem(me + o, count)
            c = pltpu.make_async_remote_copy(
                src_ref=src.at[peer], dst_ref=dst.at[me], send_sem=send_sem.at[o], recv_sem=recv_sem.at[o],
                device_id={axis: peer}, device_id_type=MESH)
            c.start()
            copies.append(c)
        dst[me] = src[me]

        def wait():
            for o in range(1, count):
                origin = lax.rem(me + count - o, count)
                c = pltpu.make_async_remote_copy(
                    src_ref=src.at[origin], dst_ref=dst.at[origin], send_sem=send_sem.at[o],
                    recv_sem=recv_sem.at[o], device_id={axis: origin}, device_id_type=MESH)
                c.wait_recv()
            for c in copies:
                c.wait_send()
        return wait

    wait = exchange("gx", mx, gx, xsend, xrecv, xs_sem, xr_sem)

    edge_lo = jnp.where(my == 0, 1.0, 0.0)
    edge_hi = jnp.where(my == gy - 1, 1.0, 0.0)
    for j in range(ny):
        gm, gp = yw[j], yw[j + 1]
        if j == 0:
            mass, link = 1.0 + edge_lo * gm, (1.0 - edge_lo) * gm
        else:
            mass, link = 1.0 + w * mass, w * link
        if j < ny - 1:
            ib = 1.0 / (mass + link + gp)
            w = gp * ib
            e = link * ib
            ye[j], yi[j], yw[j] = e, ib, w
            sig = e * mass if j == 0 else sig + e * mass
    mass = mass + edge_hi * yw[ny]
    split_send((link, mass, sig), ycs, gy, ly)
    wait_c = exchange("gy", my, gy, ycs, ycr, ycs_sem, ycr_sem)

    wait()

    def reduced_factor(recv, count):
        ws, ibs = [], []
        for i in range(count):
            total = recv[i, 1] + (recv[i + 1, 2] if i < count - 1 else 0.0)
            s = total if i == 0 else total + ws[-1] * s
            if i < count - 1:
                ib = 1.0 / (s + recv[i + 1, 0])
                ws.append(recv[i + 1, 0] * ib)
            else:
                ib = 1.0 / s
            ibs.append(ib)
        return ws, ibs

    def reduced_solve(ws, ibs, own, below, count, back):
        ds = []
        for i in range(count):
            d = own(i) + (below(i + 1) if i < count - 1 else 0.0)
            ds.append(d if i == 0 else d + ws[i - 1] * ds[-1])
        x = ds[-1] * ibs[-1]
        back[count - 1, 1] = x
        for i in range(count - 2, -1, -1):
            x = ds[i] * ibs[i] + ws[i] * x
            back[i, 1] = x
            back[i + 1, 0] = x
        back[0, 0] = jnp.zeros_like(x)

    ws, ibs = reduced_factor(xrecv, gx)
    reduced_solve(ws, ibs, lambda i: xrecv[i, 3], lambda i: xrecv[i, 4], gx, xback)
    wait = exchange("gx", mx, gx, xback, xgot, xbs_sem, xbr_sem)
    for step in (0, 1):
        zfactor(step)
    wait()

    low = joined([xgot[t, 0] for t in range(gx)])
    x = joined([xgot[t, 1] for t in range(gx)])
    for i in range(nx - 1, -1, -1):
        if i < nx - 1:
            x = xd[i] + xe[i] * low + xw[i] * x
        for h in range(2):
            rhs[h, pl.ds(i * ny, ny), :] = x[h * ny:(h + 1) * ny]

    for j in range(ny):
        d = joined([rhs[h, pl.ds(j, nx, stride=ny), :] for h in range(2)])
        dd = d if j == 0 else d + yw[j - 1] * dd
        if j < ny - 1:
            yd[j] = dd * yi[j]
            d1 = ye[j] * dd if j == 0 else d1 + ye[j] * dd
    split_send((dd, d1), yrs, gy, ly)
    wait = exchange("gy", my, gy, yrs, yrr, yrs_sem, yrr_sem)
    wait_c()
    ws, ibs = reduced_factor(ycr, gy)
    for i in range(gy):
        yfi[i] = ibs[i]
        if i < gy - 1:
            yfw[i] = ws[i]
    for step in (2, 3, 4):
        zfactor(step)
    wait()
    reduced_solve([yfw[i] for i in range(gy - 1)], [yfi[i] for i in range(gy)],
                  lambda i: yrr[i, 0], lambda i: yrr[i, 1], gy, yback)
    wait = exchange("gy", my, gy, yback, ygot, ybs_sem, ybr_sem)
    for step in (5, 6, 7):
        zfactor(step)
    wait()

    low = joined([ygot[t, 0] for t in range(gy)])
    x = joined([ygot[t, 1] for t in range(gy)])
    for j in range(ny - 1, -1, -1):
        if j < ny - 1:
            x = yd[j] + ye[j] * low + yw[j] * x
        for h in range(2):
            rhs[h, pl.ds(j, nx, stride=ny), :] = x[h * nx:(h + 1) * nx]

    for step in range(7):
        s = 1 << step
        for r in range(0, rows, block):
            at = pl.ds(r, block)
            d = [rhs[h, at, :] for h in range(2)]
            dp, dn = prev(d, s), nxt(d, s)
            for h in range(2):
                rhs[h, at, :] = d[h] + zfm[step, h, at, :] * dp[h] + zfp[step, h, at, :] * dn[h]
    for r in range(0, rows, block):
        at = pl.ds(r, block)
        d = [rhs[h, at, :] for h in range(2)]
        for h in range(2):
            rhs[h, at, :] = field[0, h, at, :] + (d[h] + zfm[7, h, at, :] * d[1 - h]) * zfp[7, h, at, :]
    stores = []
    for h in range(2):
        c = pltpu.make_async_copy(rhs.at[h], o_hbm.at[:, pl.ds(h * LANES, LANES)], out_sem.at[h])
        c.start()
        stores.append(c)
    for c in stores:
        c.wait()


def local(gx, gy, initial_warmth, energy_source_density, baseline_transport_coefficient):
    nx, ny, nz = initial_warmth.shape
    rows = nx * ny
    xr, yr = 2 * ny, 2 * nx
    lx, ly = xr // gx, yr // gy
    flat = [a.reshape(rows, nz) for a in (initial_warmth, energy_source_density, baseline_transport_coefficient)]

    def vm(*shape):
        return pltpu.VMEM(shape, jnp.float32)

    dma = pltpu.SemaphoreType.DMA
    out = pl.pallas_call(
        functools.partial(kernel, nx, ny, gx, gy, lx, ly),
        out_shape=jax.ShapeDtypeStruct((rows, nz), jnp.float32),
        in_specs=[pl.BlockSpec(memory_space=pl.ANY)] * 3,
        out_specs=pl.BlockSpec(memory_space=pl.ANY),
        scratch_shapes=[
            vm(2, 2, rows, LANES), vm(2, rows, LANES),
            vm(nx, xr, LANES), vm(nx, xr, LANES), vm(nx, xr, LANES),
            vm(ny, yr, LANES), vm(ny, yr, LANES), vm(ny + 1, yr, LANES), vm(ny, yr, LANES),
            vm(2, 2, 2, ny, LANES), vm(2, 2, 2, nx, LANES), vm(2, 2, 2, nx, LANES),
            vm(3, 2, rows, LANES), vm(8, 2, rows, LANES), vm(8, 2, rows, LANES),
            vm(gx, 5, lx, LANES), vm(gx, 5, lx, LANES), vm(gx, 2, lx, LANES), vm(gx, 2, lx, LANES),
            vm(gy, 3, ly, LANES), vm(gy, 3, ly, LANES), vm(gy, 2, ly, LANES), vm(gy, 2, ly, LANES),
            vm(gy, 2, ly, LANES), vm(gy, 2, ly, LANES),
            vm(gy, ly, LANES), vm(gy, ly, LANES),
            dma((3, 2)), dma((2,)), dma((4,)), dma((4,)),
            dma((gx,)), dma((gx,)), dma((gx,)), dma((gx,)),
            dma((gy,)), dma((gy,)), dma((gy,)), dma((gy,)), dma((gy,)), dma((gy,)),
        ],
        compiler_params=pltpu.CompilerParams(
            collective_id=0, has_side_effects=True, vmem_limit_bytes=40 * 1024 * 1024),
        name="adi_step",
    )(*flat)
    return out.reshape(nx, ny, nz)


def solution(mesh):
    spec = P("gx", "gy", None)
    return jax.shard_map(
        functools.partial(local, mesh.shape["gx"], mesh.shape["gy"]),
        mesh=mesh,
        in_specs=(spec, spec, spec),
        out_specs=spec,
        check_vma=False,
    )
```

profile of v0, /device:TPU:0, one launch (start us, length us, event | category | flops | bytes accessed | tf_op | source)
XLA Modules:
  0.0 32.0 jit_solution(17675692258273245465)
XLA Ops:
  0.0 0.0 copy-start
  0.0 1.0 %copy-done = f32[32,16,256]{2,1,0:T(8,128)S(1)} copy-done((f32[32,16,256]{2,1,0:T(8,128)S(1)}, f32[32,16,256]{2,1,0:T(8,128)}, u32[]{:S(2)}) %copy-start) | copy-done | bytes 524312
  1.0 0.0 copy-start.1
  1.0 1.0 %copy-done.1 = f32[32,16,256]{2,1,0:T(8,128)S(1)} copy-done((f32[32,16,256]{2,1,0:T(8,128)S(1)}, f32[32,16,256]{2,1,0:T(8,128)}, u32[]{:S(2)}) %copy-start.1) | copy-done | bytes 524312
  2.1 0.0 copy-start.2
  2.1 1.0 %copy-done.2 = f32[32,16,256]{2,1,0:T(8,128)S(1)} copy-done((f32[32,16,256]{2,1,0:T(8,128)S(1)}, f32[32,16,256]{2,1,0:T(8,128)}, u32[]{:S(2)}) %copy-start.2) | copy-done | bytes 524312
  3.1 28.1 %adi_step.1 = f32[512,256]{1,0:T(8,128)S(1)} custom-call(f32[512,256]{1,0:T(8,128)S(1)} %bitcast.5, f32[512,256]{1,0:T(8,128)S(1)} %bitcast.6, f32[512,256]{1,0:T(8,128)S(1)} %bitcast.7), custom_call_target="tpu_custom_call" | custom-call | tf_op jit(solution)/shard_map/adi_step/pallas_call | solution.py:370
  31.2 0.8 %copy.5 = f32[32,16,256]{2,1,0:T(8,128)} copy(f32[32,16,256]{2,1,0:T(8,128)S(1)} %bitcast.4) | data formatting | bytes 1048576
Async XLA Ops:
  0.0 1.0 %copy-start = (f32[32,16,256]{2,1,0:T(8,128)S(1)}, f32[32,16,256]{2,1,0:T(8,128)}, u32[]{:S(2)}) copy-start(f32[32,16,256]{2,1,0:T(8,128)} %param.3) | copy-start | bytes 1572868
  1.0 1.0 %copy-start.1 = (f32[32,16,256]{2,1,0:T(8,128)S(1)}, f32[32,16,256]{2,1,0:T(8,128)}, u32[]{:S(2)}) copy-start(f32[32,16,256]{2,1,0:T(8,128)} %param.4) | copy-start | bytes 1572868
  2.1 1.0 %copy-start.2 = (f32[32,16,256]{2,1,0:T(8,128)S(1)}, f32[32,16,256]{2,1,0:T(8,128)}, u32[]{:S(2)}) copy-start(f32[32,16,256]{2,1,0:T(8,128)} %param.5) | copy-start | bytes 1572868
where the time goes:
time: 32.3 us; the launch traced here: 32 us
  Pallas kernels  28.1 us (87%)
  local copies, waits for them, and re-layouts  3.92 us (12%)
    pallas_call x1, Pallas kernels, local(): pl.pallas_call(functools.partial(kernel, nx, ny, gx, gy, lx, ly), out_sha...  28.1 us
    unnamed x7, local copies, waits for them, and re-layouts  3.92 us

commit v1 on v0

v1 whole, which is shorter than its diff:
```python
import functools

import jax
import jax.numpy as jnp
from jax import lax
from jax.experimental import pallas as pl
from jax.experimental.pallas import tpu as pltpu
from jax.sharding import PartitionSpec as P

MESH = pl.DeviceIdType.MESH
LANES = 128


def kernel(nx, ny, gx, gy, ly, u_hbm, s_hbm, k_hbm, o_hbm,
           field, rhs, xd, xe, xw, xi, yd, ye, yw, yi, xz, yz, hx, hys, hyr,
           zq, zfm, zfp,
           xcs, xcr, xrs, xrr, xred, xfw, xfi, xx, ycs, ycr, yrs, yrr, yback, ygot, yfw, yfi,
           in_sem, out_sem, hs_sem, hr_sem, xcs_sem, xcr_sem, xrs_sem, xrr_sem,
           ycs_sem, ycr_sem, yrs_sem, yrr_sem, ybs_sem, ybr_sem):
    rows = nx * ny
    mx = lax.axis_index("gx")
    my = lax.axis_index("gy")

    loads = []
    for a, (src, dst) in enumerate(((u_hbm, field.at[0]), (k_hbm, field.at[1]), (s_hbm, rhs))):
        for h in range(2):
            c = pltpu.make_async_copy(src.at[:, pl.ds(h * LANES, LANES)], dst.at[h], in_sem.at[a, h])
            c.start()
            loads.append(c)

    barrier = pltpu.get_barrier_semaphore()
    for o in range(1, gx):
        pl.semaphore_signal(barrier, inc=1, device_id={"gx": lax.rem(mx + o, gx)}, device_id_type=MESH)
    for o in range(1, gy):
        pl.semaphore_signal(barrier, inc=1, device_id={"gy": lax.rem(my + o, gy)}, device_id_type=MESH)

    for c in loads[:4]:
        c.wait()
    block = 32
    for r in range(0, rows, block):
        u = field[0, :, r:r + block, :]
        field[1, :, r:r + block, :] = field[1, :, r:r + block, :] * (1.0 + 0.5 * u * u)

    for q in range(2):
        for h in range(2):
            hys[0, q, h] = field[q, h, pl.ds(0, nx, stride=ny), :]
            hys[1, q, h] = field[q, h, pl.ds(ny - 1, nx, stride=ny), :]

    for c in loads[4:]:
        c.wait()

    lane = lax.broadcasted_iota(jnp.int32, (block, LANES), 1)

    def prev(a, s):
        if s == LANES:
            return a[1], a[0]
        p0, p1 = pltpu.roll(a[0], s, 1), pltpu.roll(a[1], s, 1)
        return p0, jnp.where(lane < s, p0, p1)

    def nxt(a, s):
        n0, n1 = pltpu.roll(a[0], LANES - s, 1), pltpu.roll(a[1], LANES - s, 1)
        return jnp.where(lane >= LANES - s, n1, n0), n1

    first, last = lane == 0, lane == LANES - 1

    for r in range(0, rows, block):
        at = pl.ds(r, block)
        u = [field[0, h, at, :] for h in range(2)]
        c = [field[1, h, at, :] for h in range(2)]
        up_, cp = prev(u, 1), prev(c, 1)
        un, cn = nxt(u, 1), nxt(c, 1)
        zero = jnp.zeros_like(lane, jnp.float32)
        up_, cp = [jnp.where(first, zero, up_[0]), up_[1]], [jnp.where(first, zero, cp[0]), cp[1]]
        un, cn = [un[0], jnp.where(last, zero, un[1])], [cn[0], jnp.where(last, zero, cn[1])]
        for h in range(2):
            gm, gp = 0.25 * (c[h] + cp[h]), 0.25 * (c[h] + cn[h])
            rhs[h, at, :] = rhs[h, at, :] + 2.0 * (gp * (un[h] - u[h]) - gm * (u[h] - up_[h]))
            if h == 0:
                zq[0, h, at, :] = jnp.where(first, zero, gm)
                zq[1, h, at, :] = gp
                zq[2, h, at, :] = jnp.where(first, 1.0 + gm, 1.0)
            else:
                zq[0, h, at, :] = gm
                zq[1, h, at, :] = jnp.where(last, zero, gp)
                zq[2, h, at, :] = jnp.where(last, 1.0 + gp, 1.0)

    def zfactor(step):
        s = 1 << step
        for r in range(0, rows, block):
            at = pl.ds(r, block)
            qm = [zq[0, h, at, :] for h in range(2)]
            qp = [zq[1, h, at, :] for h in range(2)]
            m = [zq[2, h, at, :] for h in range(2)]
            ib = [1.0 / (m[h] + (qm[h] + qp[h])) for h in range(2)]
            if s == LANES:
                fp0, fm1 = qp[0] * ib[1], qm[1] * ib[0]
                zfm[step, 0, at, :] = fp0
                zfm[step, 1, at, :] = fm1
                zfp[step, 0, at, :] = 1.0 / (m[0] + fp0 * m[1])
                zfp[step, 1, at, :] = 1.0 / (m[1] + fm1 * m[0])
                continue
            ip, inx = prev(ib, s), nxt(ib, s)
            mp, mn = prev(m, s), nxt(m, s)
            qmp, qpn = prev(qm, s), nxt(qp, s)
            for h in range(2):
                fm, fp = qm[h] * ip[h], qp[h] * inx[h]
                zfm[step, h, at, :] = fm
                zfp[step, h, at, :] = fp
                zq[0, h, at, :] = fm * qmp[h]
                zq[1, h, at, :] = fp * qpn[h]
                zq[2, h, at, :] = m[h] + (fm * mp[h] + fp * mn[h])

    def joined(parts):
        return jnp.concatenate(parts, axis=0)

    def xat(i):
        return pl.ds(i * ny, ny)

    def yat(j):
        return pl.ds(j, nx, stride=ny)

    def line(ref, at):
        return joined([ref[h, at, :] for h in range(2)])

    def put_line(ref, at, v):
        half = v.shape[0] // 2
        for h in range(2):
            ref[h, at, :] = v[h * half:(h + 1) * half]

    def split_send(values, buf, count, per):
        for q, v in enumerate(values):
            for t in range(count):
                buf[t, q] = v[t * per:(t + 1) * per]

    def inner(n, at, si, se, sw):
        u, c = line(field.at[0], at(0)), line(field.at[1], at(0))
        flux = None
        for i in range(n):
            if i < n - 1:
                un, cn = line(field.at[0], at(i + 1)), line(field.at[1], at(i + 1))
                gp = 0.25 * (c + cn)
                fp = 2.0 * (gp * (un - u))
                change = fp if flux is None else fp - flux
            else:
                change = -flux
            put_line(rhs, at(i), line(rhs, at(i)) + change)
            if i == 1:
                mass, link = 1.0, gm
            elif i > 1:
                mass, link = 1.0 + w * mass, w * link
            if 0 < i < n - 1:
                ib = 1.0 / (mass + link + gp)
                w, e = gp * ib, link * ib
                si[i], se[i], sw[i] = ib, e, w
                sig = 1.0 + e * mass if i == 1 else sig + e * mass
            if i < n - 1:
                flux, u, c, gm = fp, un, cn, gp
        return sig, link, mass

    def row_zero(mass_0, link, g):
        ib = 1.0 / (mass_0 + (link + g))
        w, e = link * ib, g * ib
        return ib, w, e, w * g, w * mass_0, e * mass_0

    def sides(n, at, recv):
        out = []
        for side, i in ((0, 0), (1, n - 1)):
            un, cn = [joined([recv[side, q, 0], recv[side, q, 1]]) for q in range(2)]
            g = 0.25 * (line(field.at[1], at(i)) + cn)
            put_line(rhs, at(i), line(rhs, at(i)) + 2.0 * (g * (un - line(field.at[0], at(i)))))
            out.append(g)
        return out

    def forward(n, at, si, se, sw, sd):
        dd = line(rhs, at(1))
        for i in range(1, n - 1):
            if i > 1:
                dd = line(rhs, at(i)) + sw[i - 1] * dd
            sd[i] = dd * si[i]
            d1 = se[i] * dd if i == 1 else d1 + se[i] * dd
        return line(rhs, at(0)) + d1, line(rhs, at(n - 1)) + sw[n - 2] * dd

    def backward(n, at, se, sw, sd, x0, xl):
        put_line(rhs, at(n - 1), xl)
        x = xl
        for i in range(n - 2, 0, -1):
            x = sd[i] + se[i] * x0 + sw[i] * x
            put_line(rhs, at(i), x)
        put_line(rhs, at(0), x0)

    def halo(axis, me, count, src_first, src_last, recv, base):
        down = pltpu.make_async_remote_copy(
            src_ref=src_first, dst_ref=recv.at[1], send_sem=hs_sem.at[base], recv_sem=hr_sem.at[base],
            device_id={axis: lax.rem(me + count - 1, count)}, device_id_type=MESH)
        up = pltpu.make_async_remote_copy(
            src_ref=src_last, dst_ref=recv.at[0], send_sem=hs_sem.at[base + 1], recv_sem=hr_sem.at[base + 1],
            device_id={axis: lax.rem(me + 1, count)}, device_id_type=MESH)

        @pl.when(me > 0)
        def _():
            down.start()

        @pl.when(me < count - 1)
        def _():
            up.start()

        @pl.when(me == 0)
        def _():
            recv[0] = jnp.zeros(recv.shape[1:], jnp.float32)

        @pl.when(me == count - 1)
        def _():
            recv[1] = jnp.zeros(recv.shape[1:], jnp.float32)

        def wait():
            @pl.when(me > 0)
            def _():
                down.wait_send()
                up.wait_recv()

            @pl.when(me < count - 1)
            def _():
                up.wait_send()
                down.wait_recv()
        return wait

    def exchange(axis, me, count, src, dst, send_sem, recv_sem):
        copies = []
        for o in range(1, count):
            peer = lax.rem(me + o, count)
            c = pltpu.make_async_remote_copy(
                src_ref=src.at[peer], dst_ref=dst.at[me], send_sem=send_sem.at[o], recv_sem=recv_sem.at[o],
                device_id={axis: peer}, device_id_type=MESH)
            c.start()
            copies.append(c)
        dst[me] = src[me]

        def wait():
            for o in range(1, count):
                origin = lax.rem(me + count - o, count)
                c = pltpu.make_async_remote_copy(
                    src_ref=src.at[origin], dst_ref=dst.at[origin], send_sem=send_sem.at[o],
                    recv_sem=recv_sem.at[o], device_id={axis: origin}, device_id_type=MESH)
                c.wait_recv()
            for c in copies:
                c.wait_send()
        return wait

    def gather(axis, me, count, src, dst, send_sem, recv_sem):
        copies = []
        for o in range(1, count):
            c = pltpu.make_async_remote_copy(
                src_ref=src, dst_ref=dst.at[me], send_sem=send_sem.at[o], recv_sem=recv_sem.at[o],
                device_id={axis: lax.rem(me + o, count)}, device_id_type=MESH)
            c.start()
            copies.append(c)
        dst[me] = src[...]

        def wait():
            for o in range(1, count):
                origin = lax.rem(me + count - o, count)
                c = pltpu.make_async_remote_copy(
                    src_ref=src, dst_ref=dst.at[origin], send_sem=send_sem.at[o],
                    recv_sem=recv_sem.at[o], device_id={axis: origin}, device_id_type=MESH)
                c.wait_recv()
            for c in copies:
                c.wait_send()
        return wait

    def reduced_factor(recv, count):
        ws, ibs = [], []
        for i in range(count):
            total = recv[i, 1] + (recv[i + 1, 2] if i < count - 1 else 0.0)
            s = total if i == 0 else total + ws[-1] * s
            if i < count - 1:
                ib = 1.0 / (s + recv[i + 1, 0])
                ws.append(recv[i + 1, 0] * ib)
            else:
                ib = 1.0 / s
            ibs.append(ib)
        return ws, ibs

    def reduced_solve(ws, ibs, own, below, count, back):
        ds = []
        for i in range(count):
            d = own(i) + (below(i + 1) if i < count - 1 else 0.0)
            ds.append(d if i == 0 else d + ws[i - 1] * ds[-1])
        x = ds[-1] * ibs[-1]
        back[count - 1, 1] = x
        for i in range(count - 2, -1, -1):
            x = ds[i] * ibs[i] + ws[i] * x
            back[i, 1] = x
            back[i + 1, 0] = x
        back[0, 0] = jnp.zeros_like(x)

    x_mass_0, x_link, x_mass = inner(nx, xat, xi, xe, xw)
    xcs[0], xcs[1], xcs[2] = x_mass_0, x_link, x_mass
    xcs[3], xcs[4] = line(field.at[1], xat(0)), line(field.at[1], xat(nx - 1))

    pl.semaphore_wait(barrier, gx + gy - 2)

    wait_y = halo("gy", my, gy, hys.at[0], hys.at[1], hyr, 0)
    wait_x = halo("gx", mx, gx, field.at[:, :, pl.ds(0, ny), :],
                  field.at[:, :, pl.ds(rows - ny, ny), :], hx, 2)

    wait_xc = gather("gx", mx, gx, xcs, xcr, xcs_sem, xcr_sem)
    y_mass_0, y_link, y_mass = inner(ny, yat, yi, ye, yw)

    wait_y()
    y_low, y_high = sides(ny, yat, hyr)
    wait_x()
    x_low, x_high = sides(nx, xat, hx)

    own_lo = jnp.where(mx == 0, 1.0, 0.0)
    x_ib, x_w, x_e, _, _, _ = row_zero(x_mass_0 + own_lo * x_low, x_link, (1.0 - own_lo) * x_low)
    d0, dl = forward(nx, xat, xi, xe, xw, xd)
    xrs[0], xrs[1] = dl + x_w * d0, x_e * d0
    wait = gather("gx", mx, gx, xrs, xrr, xrs_sem, xrr_sem)
    x_d = d0 * x_ib

    own_lo = jnp.where(my == 0, 1.0, 0.0)
    own_hi = jnp.where(my == gy - 1, 1.0, 0.0)
    mass_0 = y_mass_0 + own_lo * y_low
    y_ib, y_w, y_e, link, more, sig = row_zero(mass_0, y_link, (1.0 - own_lo) * y_low)
    split_send((link, (y_mass + more) + own_hi * y_high, sig), ycs, gy, ly)
    wait_c = exchange("gy", my, gy, ycs, ycr, ycs_sem, ycr_sem)
    yz[0], yz[1], yz[2] = y_ib, y_w, y_e
    xz[0], xz[1], xz[2] = x_d, x_w, x_e

    wait_xc()
    for t in range(gx):
        m0, ml = xcr[t, 0], xcr[t, 2]
        if t == 0:
            m0 = m0 + 0.25 * xcr[t, 3]
            g = jnp.zeros_like(m0)
        else:
            g = 0.25 * (xcr[t - 1, 4] + xcr[t, 3])
        if t == gx - 1:
            ml = ml + 0.25 * xcr[t, 4]
        _, _, _, link, more, sig = row_zero(m0, xcr[t, 1], g)
        xred[t, 0], xred[t, 1], xred[t, 2] = link, ml + more, sig
    ws, ibs = reduced_factor(xred, gx)
    for i in range(gx):
        xfi[i] = ibs[i]
        if i < gx - 1:
            xfw[i] = ws[i]
    for step in (0, 1, 2):
        zfactor(step)
    wait()
    ws, ibs = [xfw[i] for i in range(gx - 1)], [xfi[i] for i in range(gx)]
    ds = []
    for i in range(gx):
        d = xrr[i, 0] + (xrr[i + 1, 1] if i < gx - 1 else 0.0)
        ds.append(d if i == 0 else d + ws[i - 1] * ds[-1])
    x = ds[-1] * ibs[-1]
    xx[gx] = x
    for i in range(gx - 2, -1, -1):
        x = ds[i] * ibs[i] + ws[i] * x
        xx[i + 1] = x
    xx[0] = jnp.zeros_like(x)

    low, xl = xx[mx], xx[mx + 1]
    backward(nx, xat, xe, xw, xd, xz[0] + xz[2] * low + xz[1] * xl, xl)

    d0, dl = forward(ny, yat, yi, ye, yw, yd)
    split_send((dl + yz[1] * d0, yz[2] * d0), yrs, gy, ly)
    wait = exchange("gy", my, gy, yrs, yrr, yrs_sem, yrr_sem)
    yz[3] = d0 * yz[0]
    wait_c()
    ws, ibs = reduced_factor(ycr, gy)
    for i in range(gy):
        yfi[i] = ibs[i]
        if i < gy - 1:
            yfw[i] = ws[i]
    for step in (3, 4, 5):
        zfactor(step)
    wait()
    reduced_solve([yfw[i] for i in range(gy - 1)], [yfi[i] for i in range(gy)],
                  lambda i: yrr[i, 0], lambda i: yrr[i, 1], gy, yback)
    wait = exchange("gy", my, gy, yback, ygot, ybs_sem, ybr_sem)
    for step in (6, 7):
        zfactor(step)
    wait()
    low = joined([ygot[t, 0] for t in range(gy)])
    xl = joined([ygot[t, 1] for t in range(gy)])
    backward(ny, yat, ye, yw, yd, yz[3] + yz[2] * low + yz[1] * xl, xl)

    for step in range(7):
        s = 1 << step
        for r in range(0, rows, block):
            at = pl.ds(r, block)
            d = [rhs[h, at, :] for h in range(2)]
            dp, dn = prev(d, s), nxt(d, s)
            for h in range(2):
                rhs[h, at, :] = d[h] + zfm[step, h, at, :] * dp[h] + zfp[step, h, at, :] * dn[h]
    for r in range(0, rows, block):
        at = pl.ds(r, block)
        d = [rhs[h, at, :] for h in range(2)]
        for h in range(2):
            rhs[h, at, :] = field[0, h, at, :] + (d[h] + zfm[7, h, at, :] * d[1 - h]) * zfp[7, h, at, :]
    stores = []
    for h in range(2):
        c = pltpu.make_async_copy(rhs.at[h], o_hbm.at[:, pl.ds(h * LANES, LANES)], out_sem.at[h])
        c.start()
        stores.append(c)
    for c in stores:
        c.wait()


def local(gx, gy, initial_warmth, energy_source_density, baseline_transport_coefficient):
    nx, ny, nz = initial_warmth.shape
    rows = nx * ny
    xr, yr = 2 * ny, 2 * nx
    ly = yr // gy
    flat = [a.reshape(rows, nz) for a in (initial_warmth, energy_source_density, baseline_transport_coefficient)]

    def vm(*shape):
        return pltpu.VMEM(shape, jnp.float32)

    dma = pltpu.SemaphoreType.DMA
    out = pl.pallas_call(
        functools.partial(kernel, nx, ny, gx, gy, ly),
        out_shape=jax.ShapeDtypeStruct((rows, nz), jnp.float32),
        in_specs=[pl.BlockSpec(memory_space=pl.ANY)] * 3,
        out_specs=pl.BlockSpec(memory_space=pl.ANY),
        scratch_shapes=[
            vm(2, 2, rows, LANES), vm(2, rows, LANES),
            vm(nx, xr, LANES), vm(nx, xr, LANES), vm(nx, xr, LANES), vm(nx, xr, LANES),
            vm(ny, yr, LANES), vm(ny, yr, LANES), vm(ny, yr, LANES), vm(ny, yr, LANES),
            vm(3, xr, LANES), vm(4, yr, LANES),
            vm(2, 2, 2, ny, LANES), vm(2, 2, 2, nx, LANES), vm(2, 2, 2, nx, LANES),
            vm(3, 2, rows, LANES), vm(8, 2, rows, LANES), vm(8, 2, rows, LANES),
            vm(5, xr, LANES), vm(gx, 5, xr, LANES), vm(2, xr, LANES), vm(gx, 2, xr, LANES),
            vm(gx, 3, xr, LANES), vm(gx, xr, LANES), vm(gx, xr, LANES), vm(gx + 1, xr, LANES),
            vm(gy, 3, ly, LANES), vm(gy, 3, ly, LANES), vm(gy, 2, ly, LANES), vm(gy, 2, ly, LANES),
            vm(gy, 2, ly, LANES), vm(gy, 2, ly, LANES),
            vm(gy, ly, LANES), vm(gy, ly, LANES),
            dma((3, 2)), dma((2,)), dma((4,)), dma((4,)),
            dma((gx,)), dma((gx,)), dma((gx,)), dma((gx,)),
            dma((gy,)), dma((gy,)), dma((gy,)), dma((gy,)), dma((gy,)), dma((gy,)),
        ],
        compiler_params=pltpu.CompilerParams(
            collective_id=0, has_side_effects=True, vmem_limit_bytes=60 * 1024 * 1024),
        name="adi_step",
    )(*flat)
    return out.reshape(nx, ny, nz)


def solution(mesh):
    spec = P("gx", "gy", None)
    return jax.shard_map(
        functools.partial(local, mesh.shape["gx"], mesh.shape["gy"]),
        mesh=mesh,
        in_specs=(spec, spec, spec),
        out_specs=spec,
        check_vma=False,
    )
```

time: 32.3 us -> 28.2 us (0.87)
  local copies, waits for them, and re-layouts: 3.92 us -> 1.87 us
  Pallas kernels: 28.1 us -> 26.1 us
    unnamed x7 -> x1, local copies, waits for them, and re-layouts: 3.92 us -> 1.87 us
    pallas_call x1, Pallas kernels: 28.1 us -> 26.1 us  [local(): pl.pallas_call(functools.partial(kernel, nx, ny, gx, gy, ly), out_shape=j...]
where the time goes in v1:
time: 28.2 us; the launch traced here: 28 us
  Pallas kernels  26.1 us (93%)
  local copies, waits for them, and re-layouts  1.87 us (7%)
    pallas_call x1, Pallas kernels, local(): pl.pallas_call(functools.partial(kernel, nx, ny, gx, gy, ly), out_shape=j...  26.1 us
    unnamed x1, local copies, waits for them, and re-layouts  1.87 us

profile of v1, /device:TPU:0, one launch (start us, length us, event | category | flops | bytes accessed | tf_op | source)
XLA Modules:
  0.0 28.0 jit_solution(17145835781075888081)
XLA Ops:
  0.0 26.1 %adi_step.1 = f32[512,256]{1,0:T(8,128)} custom-call(f32[512,256]{1,0:T(8,128)} %bitcast.5, f32[512,256]{1,0:T(8,128)} %bitcast.6, f32[512,256]{1,0:T(8,128)} %bitcast.7), custom_call_target="tpu_custom_call" | custom-call | tf_op jit(solution)/shard_map/adi_step/pallas_call | solution.py:421
  26.1 1.9 %copy.5 = f32[32,16,256]{2,1,0:T(8,128)} copy(f32[32,16,256]{2,1,0:T(8,128)} %bitcast.4) | data formatting | bytes 1048576
